TPU v7x, 512 devices: a whole 4x8x8 slice. The times are simulated.
512 devices in a mesh: dp: 64 (over z, x, core), seq: 8 (over y).
Axes of the slice: x: 4, y: 8, z: 8, core: 2. Of those that a mesh axis runs over, the one named last changes fastest.
Arguments:
- queries: bfloat16 [65536, 4096], P(('dp', 'seq')), may hold values from -6 to 6
- keys: bfloat16 [65536, 512], P(('dp', 'seq')), may hold values from -6 to 6
- values: bfloat16 [65536, 512], P(('dp', 'seq')), may hold values from -6 to 6
- grad_out: bfloat16 [65536, 4096], P(('dp', 'seq')), may hold values from -6 to 6
- quant_scale: float32 [2, 4, 128], replicated, may hold values from 2 to 8
- doc_lengths: int32 [64, 8], P('dp'), may hold values from 1 to 512, as said below
Outputs:
- attn_out: bfloat16 [65536, 4096], P(('dp', 'seq'))
- grad_queries: bfloat16 [65536, 4096], P(('dp', 'seq'))
- grad_keys: bfloat16 [65536, 512], P(('dp', 'seq'))
- grad_values: bfloat16 [65536, 512], P(('dp', 'seq'))
- grad_scale: float32 [2, 4, 128], replicated
Inputs may be any that keep to these rules, and one draw needn't show every extreme that they name: `doc_lengths`: each row sums to 1024; its largest length is exactly 512.
All inputs are finite; a program needn't handle non-finite values.
Results may differ from a plain program's by a relative error of at most 0.04.
Values may be sent and summed in bfloat16 or wider, within the bound.
A program may use at most 64 MiB of HBM per device.

v0:
```python
import math
import jax
import jax.numpy as jnp
from jax import lax
from jax.sharding import PartitionSpec as P

two_pi = 2.0 * math.pi


def quantize(source, clip):
    level = 127.0 * jnp.tanh(source / clip)
    return clip / 127.0 * (level - jnp.sin(two_pi * level) / two_pi)


def quant_pair(key_raw, value_raw, clip):
    return (quantize(key_raw, clip[0]), quantize(value_raw, clip[1]))


def segments(lengths, length):
    ends = jnp.cumsum(lengths)
    positions = jnp.arange(length, dtype=jnp.int32)
    return jnp.sum((positions[:, None] >= ends[None, :]).astype(jnp.int32), axis=1)


def attend(query_rows, key_rows, value_rows, grad_rows, segment, row_start, local_kv):
    length = query_rows.shape[0]
    key_len = key_rows.shape[0]
    head_dim = key_rows.shape[1] // local_kv
    per_group = query_rows.shape[1] // (local_kv * head_dim)
    query4 = query_rows.reshape(length, local_kv, per_group, head_dim)
    grad4 = grad_rows.reshape(length, local_kv, per_group, head_dim)
    key3 = key_rows.reshape(key_len, local_kv, head_dim)
    value3 = value_rows.reshape(key_len, local_kv, head_dim)
    block = min(512, length)
    scale = head_dim ** (-0.5)
    columns = jnp.arange(key_len, dtype=jnp.int32)

    def step(carry, index):
        key_acc, value_acc = carry
        start = index * block
        query_blk = lax.dynamic_slice_in_dim(query4, start, block, 0)
        grad_blk = lax.dynamic_slice_in_dim(grad4, start, block, 0)
        row_ids = row_start + start + jnp.arange(block, dtype=jnp.int32)
        row_seg = lax.dynamic_slice_in_dim(segment, row_start + start, block, 0)
        allowed = (columns[None, :] <= row_ids[:, None]) & (segment[None, :] == row_seg[:, None])
        scores = (
            jnp.einsum("qngd,knd->ngqk", query_blk, key3, preferred_element_type=jnp.float32)
            * scale
        )
        scores = jnp.where(allowed, scores, -1e30)
        weights = jnp.exp(scores - jnp.max(scores, axis=-1, keepdims=True))
        probs = weights / jnp.sum(weights, axis=-1, keepdims=True)
        probs_b = probs.astype(jnp.bfloat16)
        output = jnp.einsum(
            "ngqk,knd->qngd", probs_b, value3, preferred_element_type=jnp.float32
        ).astype(jnp.bfloat16)
        delta = jnp.transpose(
            jnp.sum(grad_blk.astype(jnp.float32) * output.astype(jnp.float32), axis=-1), (1, 2, 0)
        )
        dprob = jnp.einsum("qngd,knd->ngqk", grad_blk, value3, preferred_element_type=jnp.float32)
        dscore = (probs * (dprob - delta[..., None]) * scale).astype(jnp.bfloat16)
        grad_query = jnp.einsum(
            "ngqk,knd->qngd", dscore, key3, preferred_element_type=jnp.float32
        ).astype(jnp.bfloat16)
        key_acc = key_acc + jnp.einsum(
            "ngqk,qngd->knd", dscore, query_blk, preferred_element_type=jnp.float32
        )
        value_acc = value_acc + jnp.einsum(
            "ngqk,qngd->knd", probs_b, grad_blk, preferred_element_type=jnp.float32
        )
        return ((key_acc, value_acc), (output, grad_query))

    zeros = jnp.zeros((key_len, local_kv, head_dim), jnp.float32)
    (key_grad, value_grad), (outputs, grad_query) = lax.scan(
        step, (zeros, zeros), jnp.arange(length // block, dtype=jnp.int32)
    )
    return (
        outputs.reshape(length, -1),
        grad_query.reshape(length, -1),
        key_grad.reshape(key_len, -1),
        value_grad.reshape(key_len, -1),
    )


def on_device(queries, keys, values, grad_out, quant_scale, doc_lengths):
    tok_rows = queries.shape[0]
    seq_count = lax.axis_size("seq")
    kv_heads = quant_scale.shape[1]
    head_dim = quant_scale.shape[2]
    slab_rows = tok_rows * seq_count
    segment = segments(doc_lengths[0], slab_rows)
    key_raw = keys.astype(jnp.float32).reshape(tok_rows, kv_heads, head_dim)
    value_raw = values.astype(jnp.float32).reshape(tok_rows, kv_heads, head_dim)
    (key_q, value_q), pull_tokens = jax.vjp(quant_pair, key_raw, value_raw, quant_scale)
    send_key = key_q.astype(jnp.bfloat16).reshape(tok_rows, kv_heads * head_dim)
    send_value = value_q.astype(jnp.bfloat16).reshape(tok_rows, kv_heads * head_dim)
    repeats = max(1, seq_count // kv_heads)
    local_kv = max(1, kv_heads // seq_count)
    query_h, grad_h = (
        lax.all_to_all(queries, "seq", split_axis=1, concat_axis=0, tiled=True),
        lax.all_to_all(grad_out, "seq", split_axis=1, concat_axis=0, tiled=True),
    )

    def widen(array):
        spread = jnp.broadcast_to(
            array.reshape(tok_rows, kv_heads, 1, head_dim), (tok_rows, kv_heads, repeats, head_dim)
        )
        return spread.reshape(tok_rows, kv_heads * repeats * head_dim)

    send_key = widen(send_key)
    send_value = widen(send_value)
    key_h, value_h = (
        lax.all_to_all(send_key, "seq", split_axis=1, concat_axis=0, tiled=True),
        lax.all_to_all(send_value, "seq", split_axis=1, concat_axis=0, tiled=True),
    )
    output_h, grad_query_h, key_grad_h, value_grad_h = attend(
        query_h, key_h, value_h, grad_h, segment, 0, local_kv
    )
    attn_out, grad_queries = (
        lax.all_to_all(output_h, "seq", split_axis=0, concat_axis=1, tiled=True),
        lax.all_to_all(grad_query_h, "seq", split_axis=0, concat_axis=1, tiled=True),
    )
    key_gathered, value_gathered = (
        lax.all_to_all(key_grad_h, "seq", split_axis=0, concat_axis=1, tiled=True),
        lax.all_to_all(value_grad_h, "seq", split_axis=0, concat_axis=1, tiled=True),
    )
    key_sum = jnp.sum(key_gathered.reshape(tok_rows, kv_heads, repeats, head_dim), axis=2)
    value_sum = jnp.sum(value_gathered.reshape(tok_rows, kv_heads, repeats, head_dim), axis=2)
    key_in, value_in, scale_part = pull_tokens((key_sum, value_sum))
    grad_scale = lax.psum(scale_part, ("dp", "seq"))
    grad_keys = key_in.reshape(tok_rows, kv_heads * head_dim).astype(jnp.bfloat16)
    grad_values = value_in.reshape(tok_rows, kv_heads * head_dim).astype(jnp.bfloat16)
    return (attn_out, grad_queries, grad_keys, grad_values, grad_scale)


def solution(mesh):
    return jax.shard_map(
        on_device,
        mesh=mesh,
        in_specs=(
            P(("dp", "seq"), None),
            P(("dp", "seq"), None),
            P(("dp", "seq"), None),
            P(("dp", "seq"), None),
            P(),
            P("dp", None),
        ),
        out_specs=(
            P(("dp", "seq"), None),
            P(("dp", "seq"), None),
            P(("dp", "seq"), None),
            P(("dp", "seq"), None),
            P(),
        ),
        check_vma=False,
    )
```

profile of v0, /device:TPU:27, one launch (start us, length us, event | category | flops | bytes accessed | tf_op | source)
XLA Modules:
  0.0 368.5 jit_solution(9301017761768875349)
XLA Ops:
  0.7 1.3 multiply_bitcast_fusion
  2.0 1.0 copy.107
  3.0 1.0 multiply_convert_fusion
  4.1 0.7 broadcast_in_dim.22
  4.8 6.8 %all-to-all-start.3 = ((bf16[128,8,128]{0,2,1:T(8,128)(2,1)}), bf16[128,8,128]{0,2,1:T(8,128)(2,1)S(1)}, u32[]{:S(2)}, u32[]{:S(2)}) async-start(bf16[128,8,128]{0,2,1:T(8,128)(2,1)} %bitcast.15), calls=%async_computation.3 | async-start | bytes 524288 | tf_op jit(solution)/shard_map/all_to_all | solution.py:114
  11.6 2.3 copy.101
  13.8 5.6 %all-to-all-done.3 = bf16[128,8,128]{0,2,1:T(8,128)(2,1)S(1)} async-done(((bf16[128,8,128]{0,2,1:T(8,128)(2,1)}), bf16[128,8,128]{0,2,1:T(8,128)(2,1)S(1)}, u32[]{:S(2)}, u32[]{:S(2)}) %all-to-all-start.3) | async-done | bytes 262176 | tf_op jit(solution)/shard_map/all_to_all | solution.py:114
  19.4 6.0 %all-to-all-start = ((bf16[128,8,512]{0,2,1:T(8,128)(2,1)}), bf16[128,8,512]{0,2,1:T(8,128)(2,1)S(1)}, u32[]{:S(2)}, u32[]{:S(2)}) async-start(bf16[128,8,512]{0,2,1:T(8,128)(2,1)} %bitcast), calls=%async_computation | async-start | bytes 2097152 | tf_op jit(solution)/shard_map/all_to_all | solution.py:100
  25.4 2.3 copy.105
  27.7 19.0 %all-to-all-done = bf16[128,8,512]{0,2,1:T(8,128)(2,1)S(1)} async-done(((bf16[128,8,512]{0,2,1:T(8,128)(2,1)}), bf16[128,8,512]{0,2,1:T(8,128)(2,1)S(1)}, u32[]{:S(2)}, u32[]{:S(2)}) %all-to-all-start) | async-done | bytes 1048608 | tf_op jit(solution)/shard_map/all_to_all | solution.py:100
  46.6 9.7 %all-to-all-start.2 = ((bf16[128,8,512]{0,2,1:T(8,128)(2,1)}), bf16[128,8,512]{0,2,1:T(8,128)(2,1)S(1)}, u32[]{:S(2)}, u32[]{:S(2)}) async-start(bf16[128,8,512]{0,2,1:T(8,128)(2,1)} %bitcast.263), calls=%async_computation.2 | async-start | bytes 2097152 | tf_op jit(solution)/shard_map/all_to_all | solution.py:101
  56.5 1.0 multiply_convert_fusion.1
  57.7 20.1 %all-to-all-done.2 = bf16[128,8,512]{0,2,1:T(8,128)(2,1)S(1)} async-done(((bf16[128,8,512]{0,2,1:T(8,128)(2,1)}), bf16[128,8,512]{0,2,1:T(8,128)(2,1)S(1)}, u32[]{:S(2)}, u32[]{:S(2)}) %all-to-all-start.2) | async-done | bytes 1048608 | tf_op jit(solution)/shard_map/all_to_all | solution.py:101
  77.8 0.7 broadcast_in_dim.21
  78.5 11.1 %all-to-all-start.1 = ((bf16[128,8,128]{2,0,1:T(8,128)(2,1)}), bf16[128,8,128]{2,0,1:T(8,128)(2,1)S(1)}, u32[]{:S(2)}, u32[]{:S(2)}) async-start(bf16[128,8,128]{2,0,1:T(8,128)(2,1)} %bitcast.7), calls=%async_computation.1 | async-start | bytes 524288 | tf_op jit(solution)/shard_map/all_to_all | solution.py:113
  90.3 1.6 copy.102
  91.9 1.5 reshape.291
  93.5 1.6 copy.106
  95.1 2.3 reshape.296
  97.8 60.3 %while.17 = (s32[]{:T(128)}, f32[1024,1,128]{0,2,1:T(8,128)S(1)}, f32[1024,1,128]{0,2,1:T(8,128)}, bf16[2,512,1,4,128]{4,3,1,0,2:T(4,128)(2,1)}, bf16[2,512,1,4,...) while((s32[]{:T(128)}, f32[1024,1,128]{0,2,1:T(8,128)S(1)}, ...), condition=%wide.region_6.7_spmd.clone, body=%wide.region_2.6_spmd.clone.sunk | while | flops 3277318656 | bytes 84515176 | solution.py:74
  97.8 0.6 dynamic_slice.48
  99.1 0.5 fusion.72
  99.6 1.9 fusion.73
  101.5 2.5 fusion.74
  103.9 4.7 %fusion.77 = f32[1024,1,128]{0,2,1:T(8,128)} fusion(f32[1024,1,128]{0,2,1:T(8,128)} %get-tuple-element.341, bf16[1024,1,4,128]{0,3,2,1:T(8,128)(2,1)} %get-tuple-element.363, s32[]{:T(128)S(6)} %select_n.41, pred[]{:T(512)S(6)} %compare.5, f32[4,512]{1,0:T(4,128)S(1)} %fusion.74, f32[4,512]{1,0:T(4,128)S(1)} %get-tuple-element.319, ...), kind=kOutput, calls=%fused_computation.22.clone.1 | convolution fusion | flops 547618816 | bytes 10502149 | tf_op jit(solution)/shard_map/while/body/eval_jaxpr/ngqk,qngd->knd/dot_general | solution.py:68
  108.6 4.3 %multiply_reduce_fusion.4 = (f32[512,4]{0,1:T(4,128)S(1)}, bf16[4,512,128]{1,2,0:T(8,128)(2,1)S(1)}) fusion(bf16[1024,1,4,128]{0,3,2,1:T(8,128)(2,1)} %get-tuple-element.363, s32[]{:T(128)S(6)} %select_n.41, bf16[1024,1,128]{0,2,1:T(8,128)(2,1)S(1)} %get-tuple-element.364, f32[4,512]{1,0:T(4,128)S(1)} %fusion.74, ...), kind=kOutput, calls=%fused_computation.25.clone.1 | convolution fusion | flops 548665344 | bytes 10248196 | tf_op jit(solution)/shard_map/while/body/eval_jaxpr/ngqk,knd->qngd/dot_general | solution.py:54
  112.9 5.9 %fusion.75 = bf16[4,512,1024]{2,1,0:T(8,128)(2,1)} fusion(f32[4,512]{1,0:T(4,128)S(1)} %bitcast.273, f32[4,512]{1,0:T(4,128)S(1)} %fusion.74, f32[4,512]{1,0:T(4,128)S(1)} %get-tuple-element.319, f32[512,4,1024]{2,0,1:T(8,128)S(1)} %get-tuple-element.318, pred[512,1024]{1,0:T(8,128)(4,1)S(1)} %fusion.72, ...), kind=kOutput, calls=%fused_computation.10.clone.1 | convolution fusion | flops 553648128 | bytes 13918212 | tf_op jit(solution)/shard_map/while/body/eval_jaxpr/qngd,knd->ngqk/dot_general | solution.py:60
  119.2 3.2 fusion.76
  122.3 3.4 fusion.78
  125.8 0.7 copy_dynamic-update-slice_fusion.2
  126.5 0.9 copy-done.5
  127.5 0.3 copy-done.7
  127.8 0.6 dynamic_slice.48
  129.1 0.5 fusion.72
  129.6 1.9 fusion.73
  131.5 2.5 fusion.74
  134.0 4.9 %fusion.77 = f32[1024,1,128]{0,2,1:T(8,128)} fusion(f32[1024,1,128]{0,2,1:T(8,128)} %get-tuple-element.341, bf16[1024,1,4,128]{0,3,2,1:T(8,128)(2,1)} %get-tuple-element.363, s32[]{:T(128)S(6)} %select_n.41, pred[]{:T(512)S(6)} %compare.5, f32[4,512]{1,0:T(4,128)S(1)} %fusion.74, f32[4,512]{1,0:T(4,128)S(1)} %get-tuple-element.319, ...), kind=kOutput, calls=%fused_computation.22.clone.1 | convolution fusion | flops 547618816 | bytes 10502149 | tf_op jit(solution)/shard_map/while/body/eval_jaxpr/ngqk,qngd->knd/dot_general | solution.py:68
  138.8 4.3 %multiply_reduce_fusion.4 = (f32[512,4]{0,1:T(4,128)S(1)}, bf16[4,512,128]{1,2,0:T(8,128)(2,1)S(1)}) fusion(bf16[1024,1,4,128]{0,3,2,1:T(8,128)(2,1)} %get-tuple-element.363, s32[]{:T(128)S(6)} %select_n.41, bf16[1024,1,128]{0,2,1:T(8,128)(2,1)S(1)} %get-tuple-element.364, f32[4,512]{1,0:T(4,128)S(1)} %fusion.74, ...), kind=kOutput, calls=%fused_computation.25.clone.1 | convolution fusion | flops 548665344 | bytes 10248196 | tf_op jit(solution)/shard_map/while/body/eval_jaxpr/ngqk,knd->qngd/dot_general | solution.py:54
  143.2 5.9 %fusion.75 = bf16[4,512,1024]{2,1,0:T(8,128)(2,1)} fusion(f32[4,512]{1,0:T(4,128)S(1)} %bitcast.273, f32[4,512]{1,0:T(4,128)S(1)} %fusion.74, f32[4,512]{1,0:T(4,128)S(1)} %get-tuple-element.319, f32[512,4,1024]{2,0,1:T(8,128)S(1)} %get-tuple-element.318, pred[512,1024]{1,0:T(8,128)(4,1)S(1)} %fusion.72, ...), kind=kOutput, calls=%fused_computation.10.clone.1 | convolution fusion | flops 553648128 | bytes 13918212 | tf_op jit(solution)/shard_map/while/body/eval_jaxpr/qngd,knd->ngqk/dot_general | solution.py:60
  149.4 3.2 fusion.76
  152.6 3.4 fusion.78
  156.0 0.7 copy_dynamic-update-slice_fusion.2
  156.7 0.9 copy-done.5
  157.7 0.3 copy-done.7
  158.3 1.0 copy.117
  159.3 7.3 %all-to-all-start.6 = ((f32[8,128,128]{1,2,0:T(8,128)}), f32[8,128,128]{1,2,0:T(8,128)S(1)}, u32[]{:S(2)}, u32[]{:S(2)}) async-start(f32[8,128,128]{1,2,0:T(8,128)} %copy.117), calls=%async_computation.6 | async-start | bytes 1048576 | tf_op jit(solution)/shard_map/all_to_all | solution.py:124
  166.6 1.2 copy.120
  167.9 1.0 copy.121
  168.9 10.2 %all-to-all-done.6 = f32[8,128,128]{1,2,0:T(8,128)S(1)} async-done(((f32[8,128,128]{1,2,0:T(8,128)}), f32[8,128,128]{1,2,0:T(8,128)S(1)}, u32[]{:S(2)}, u32[]{:S(2)}) %all-to-all-start.6) | async-done | bytes 524320 | tf_op jit(solution)/shard_map/all_to_all | solution.py:124
  179.1 9.1 %all-to-all-start.7 = ((f32[8,128,128]{1,2,0:T(8,128)}), f32[8,128,128]{1,2,0:T(8,128)S(1)}, u32[]{:S(2)}, u32[]{:S(2)}) async-start(f32[8,128,128]{1,2,0:T(8,128)} %copy.121), calls=%async_computation.7 | async-start | bytes 1048576 | tf_op jit(solution)/shard_map/all_to_all | solution.py:125
  188.2 2.2 all_to_all.116
  190.5 10.2 %all-to-all-done.7 = f32[8,128,128]{1,2,0:T(8,128)S(1)} async-done(((f32[8,128,128]{1,2,0:T(8,128)}), f32[8,128,128]{1,2,0:T(8,128)S(1)}, u32[]{:S(2)}, u32[]{:S(2)}) %all-to-all-start.7) | async-done | bytes 524320 | tf_op jit(solution)/shard_map/all_to_all | solution.py:125
  200.6 9.0 %all-to-all-start.5 = ((bf16[8,128,512]{2,1,0:T(8,128)(2,1)}), bf16[8,128,512]{2,1,0:T(8,128)(2,1)S(1)}, u32[]{:S(2)}, u32[]{:S(2)}) async-start(bf16[8,128,512]{2,1,0:T(8,128)(2,1)} %all_to_all.116), calls=%async_computation.5 | async-start | bytes 2097152 | tf_op jit(solution)/shard_map/all_to_all | solution.py:121
  209.7 1.2 all_to_all.112
  210.9 22.4 %all-to-all-done.5 = bf16[8,128,512]{2,1,0:T(8,128)(2,1)S(1)} async-done(((bf16[8,128,512]{2,1,0:T(8,128)(2,1)}), bf16[8,128,512]{2,1,0:T(8,128)(2,1)S(1)}, u32[]{:S(2)}, u32[]{:S(2)}) %all-to-all-start.5) | async-done | bytes 1048608 | tf_op jit(solution)/shard_map/all_to_all | solution.py:121
  233.3 9.1 %all-to-all-start.4 = ((bf16[8,128,512]{2,1,0:T(8,128)(2,1)}), bf16[8,128,512]{2,1,0:T(8,128)(2,1)S(1)}, u32[]{:S(2)}, u32[]{:S(2)}) async-start(bf16[8,128,512]{2,1,0:T(8,128)(2,1)} %all_to_all.112), calls=%async_computation.4 | async-start | bytes 2097152 | tf_op jit(solution)/shard_map/all_to_all | solution.py:120
  242.5 2.8 fusion.45
  245.5 0.8 copy.127
  246.5 0.8 copy.126
  247.2 117.3 %psum.7 = f32[2,4,128]{2,1,0:T(4,128)} all-reduce(f32[2,4,128]{2,1,0:T(4,128)S(1)} %pad_add_fusion), channel_id=1, replica_groups=mesh['dp'=64,'seq'=8] {'dp','seq'}, use_global_device_ids=true, to_apply=%region_13.14 | all-reduce | flops 1024 | bytes 8192 | tf_op jit(solution)/shard_map/psum | solution.py:130
  364.5 0.7 copy.115
  365.2 1.3 copy.125
  366.5 0.7 copy.113
  367.2 1.3 copy.124
  (65 shorter events, 2.6 us)
Async XLA Ops:
  0.6 55.7 %copy-start.9 = (bf16[128,512]{1,0:T(8,128)(2,1)S(1)}, bf16[128,512]{1,0:T(8,128)(2,1)}, u32[]{:S(2)}) copy-start(bf16[128,512]{1,0:T(8,128)(2,1)} %param.9) | copy-start | bytes 393220
  0.6 89.0 %copy-start.16 = (s32[1,8]{1,0:T(1,128)S(1)}, s32[1,8]{1,0:T(1,128)}, u32[]{:S(2)}) copy-start(s32[1,8]{1,0:T(1,128)} %param.13) | copy-start | bytes 100
  3.0 86.6 %copy-start = (bf16[128,512]{0,1:T(8,128)(2,1)}, bf16[128,512]{0,1:T(8,128)(2,1)S(1)}, u32[]{:S(2)}) copy-start(bf16[128,512]{0,1:T(8,128)(2,1)S(1)} %copy.107) | copy-start | bytes 393220
  4.8 14.6 %all-to-all-start.3 = ((bf16[128,8,128]{0,2,1:T(8,128)(2,1)}), bf16[128,8,128]{0,2,1:T(8,128)(2,1)S(1)}, u32[]{:S(2)}, u32[]{:S(2)}) async-start(bf16[128,8,128]{0,2,1:T(8,128)(2,1)} %bitcast.15), calls=%async_computation.3 | async-start | bytes 524288 | tf_op jit(solution)/shard_map/all_to_all | solution.py:114
  19.4 27.2 %all-to-all-start = ((bf16[128,8,512]{0,2,1:T(8,128)(2,1)}), bf16[128,8,512]{0,2,1:T(8,128)(2,1)S(1)}, u32[]{:S(2)}, u32[]{:S(2)}) async-start(bf16[128,8,512]{0,2,1:T(8,128)(2,1)} %bitcast), calls=%async_computation | async-start | bytes 2097152 | tf_op jit(solution)/shard_map/all_to_all | solution.py:100
  46.6 31.2 %all-to-all-start.2 = ((bf16[128,8,512]{0,2,1:T(8,128)(2,1)}), bf16[128,8,512]{0,2,1:T(8,128)(2,1)S(1)}, u32[]{:S(2)}, u32[]{:S(2)}) async-start(bf16[128,8,512]{0,2,1:T(8,128)(2,1)} %bitcast.263), calls=%async_computation.2 | async-start | bytes 2097152 | tf_op jit(solution)/shard_map/all_to_all | solution.py:101
  56.5 33.1 %copy-start.2 = (bf16[128,512]{0,1:T(8,128)(2,1)}, bf16[128,512]{0,1:T(8,128)(2,1)S(1)}, u32[]{:S(2)}) copy-start(bf16[128,512]{0,1:T(8,128)(2,1)S(1)} %copy.103) | copy-start | bytes 393220
  78.5 19.2 %all-to-all-start.1 = ((bf16[128,8,128]{2,0,1:T(8,128)(2,1)}), bf16[128,8,128]{2,0,1:T(8,128)(2,1)S(1)}, u32[]{:S(2)}, u32[]{:S(2)}) async-start(bf16[128,8,128]{2,0,1:T(8,128)(2,1)} %bitcast.7), calls=%async_computation.1 | async-start | bytes 524288 | tf_op jit(solution)/shard_map/all_to_all | solution.py:113
  119.2 6.6 %copy-start.4 = (bf16[2,512,1,4,128]{4,3,1,0,2:T(4,128)(2,1)S(1)}, bf16[2,512,1,4,128]{4,3,1,0,2:T(4,128)(2,1)}, u32[]{:S(2)}) copy-start(bf16[2,512,1,4,128]{4,3,1,0,2:T(4,128)(2,1)} %get-tuple-element.343) | copy-start | bytes 3145732 | tf_op jit(solution)/shard_map/while
  119.2 6.6 %copy-start.6 = (bf16[2,512,1,4,128]{4,3,1,0,2:T(4,128)(2,1)S(1)}, bf16[2,512,1,4,128]{4,3,1,0,2:T(4,128)(2,1)}, u32[]{:S(2)}) copy-start(bf16[2,512,1,4,128]{4,3,1,0,2:T(4,128)(2,1)} %get-tuple-element.342) | copy-start | bytes 3145732 | tf_op jit(solution)/shard_map/while
  126.5 1.0 copy-start.5
  126.5 1.3 copy-start.7
  149.4 6.6 %copy-start.4 = (bf16[2,512,1,4,128]{4,3,1,0,2:T(4,128)(2,1)S(1)}, bf16[2,512,1,4,128]{4,3,1,0,2:T(4,128)(2,1)}, u32[]{:S(2)}) copy-start(bf16[2,512,1,4,128]{4,3,1,0,2:T(4,128)(2,1)} %get-tuple-element.343) | copy-start | bytes 3145732 | tf_op jit(solution)/shard_map/while
  149.4 6.6 %copy-start.6 = (bf16[2,512,1,4,128]{4,3,1,0,2:T(4,128)(2,1)S(1)}, bf16[2,512,1,4,128]{4,3,1,0,2:T(4,128)(2,1)}, u32[]{:S(2)}) copy-start(bf16[2,512,1,4,128]{4,3,1,0,2:T(4,128)(2,1)} %get-tuple-element.342) | copy-start | bytes 3145732 | tf_op jit(solution)/shard_map/while
  156.7 1.0 copy-start.5
  156.7 1.3 copy-start.7
  158.0 51.6 %copy-start.8 = (bf16[2,512,1,4,128]{4,3,1,0,2:T(4,128)(2,1)S(1)}, bf16[2,512,1,4,128]{4,3,1,0,2:T(4,128)(2,1)}, u32[]{:S(2)}) copy-start(bf16[2,512,1,4,128]{4,3,1,0,2:T(4,128)(2,1)} %get-tuple-element.70) | copy-start | bytes 3145732
  158.0 84.4 %copy-start.1 = (bf16[128,512]{0,1:T(8,128)(2,1)S(1)}, bf16[128,512]{0,1:T(8,128)(2,1)}, u32[]{:S(2)}) copy-start(bf16[128,512]{0,1:T(8,128)(2,1)} %copy-done) | copy-start | bytes 393220
  158.0 84.4 %copy-start.3 = (bf16[128,512]{0,1:T(8,128)(2,1)S(1)}, bf16[128,512]{0,1:T(8,128)(2,1)}, u32[]{:S(2)}) copy-start(bf16[128,512]{0,1:T(8,128)(2,1)} %copy-done.2) | copy-start | bytes 393220
  158.0 84.4 %copy-start.10 = (f32[512]{0:T(512)S(1)}, f32[512]{0:T(512)}, u32[]{:S(2)}) copy-start(f32[512]{0:T(512)} %get-tuple-element.234) | copy-start | bytes 6148
  158.0 84.4 %copy-start.11 = (f32[512]{0:T(512)S(1)}, f32[512]{0:T(512)}, u32[]{:S(2)}) copy-start(f32[512]{0:T(512)} %get-tuple-element.238) | copy-start | bytes 6148
  158.1 84.4 %copy-start.12 = (f32[512]{0:T(512)S(1)}, f32[512]{0:T(512)}, u32[]{:S(2)}) copy-start(f32[512]{0:T(512)} %get-tuple-element.232) | copy-start | bytes 6148
  158.1 84.4 %copy-start.13 = (f32[512]{0:T(512)S(1)}, f32[512]{0:T(512)}, u32[]{:S(2)}) copy-start(f32[512]{0:T(512)} %get-tuple-element.235) | copy-start | bytes 6148
  158.1 84.4 %copy-start.14 = (f32[512]{0:T(512)S(1)}, f32[512]{0:T(512)}, u32[]{:S(2)}) copy-start(f32[512]{0:T(512)} %get-tuple-element.236) | copy-start | bytes 6148
  158.1 84.4 %copy-start.15 = (f32[512]{0:T(512)S(1)}, f32[512]{0:T(512)}, u32[]{:S(2)}) copy-start(f32[512]{0:T(512)} %get-tuple-element.239) | copy-start | bytes 6148
  159.3 19.8 %all-to-all-start.6 = ((f32[8,128,128]{1,2,0:T(8,128)}), f32[8,128,128]{1,2,0:T(8,128)S(1)}, u32[]{:S(2)}, u32[]{:S(2)}) async-start(f32[8,128,128]{1,2,0:T(8,128)} %copy.117), calls=%async_computation.6 | async-start | bytes 1048576 | tf_op jit(solution)/shard_map/all_to_all | solution.py:124
  179.1 21.5 %all-to-all-start.7 = ((f32[8,128,128]{1,2,0:T(8,128)}), f32[8,128,128]{1,2,0:T(8,128)S(1)}, u32[]{:S(2)}, u32[]{:S(2)}) async-start(f32[8,128,128]{1,2,0:T(8,128)} %copy.121), calls=%async_computation.7 | async-start | bytes 1048576 | tf_op jit(solution)/shard_map/all_to_all | solution.py:125
  200.6 32.7 %all-to-all-start.5 = ((bf16[8,128,512]{2,1,0:T(8,128)(2,1)}), bf16[8,128,512]{2,1,0:T(8,128)(2,1)S(1)}, u32[]{:S(2)}, u32[]{:S(2)}) async-start(bf16[8,128,512]{2,1,0:T(8,128)(2,1)} %all_to_all.116), calls=%async_computation.5 | async-start | bytes 2097152 | tf_op jit(solution)/shard_map/all_to_all | solution.py:121
  233.3 133.2 %all-to-all-start.4 = ((bf16[8,128,512]{2,1,0:T(8,128)(2,1)}), bf16[8,128,512]{2,1,0:T(8,128)(2,1)S(1)}, u32[]{:S(2)}, u32[]{:S(2)}) async-start(bf16[8,128,512]{2,1,0:T(8,128)(2,1)} %all_to_all.112), calls=%async_computation.4 | async-start | bytes 2097152 | tf_op jit(solution)/shard_map/all_to_all | solution.py:120
where the time goes:
time: 370 us; the launch traced here: 368 us
  blocking collectives  117 us (32%)
  waiting for transfers between devices  87.9 us (24%)
  starting transfers between devices  68.1 us (18%)
  matrix products  46.9 us (13%)
  local copies, waits for them, and re-layouts  33.1 us (9%)
  other arithmetic  12.8 us (3%)
    psum x1, blocking collectives, on_device(): grad_scale = lax.psum(scale_part, ('dp', 'seq'))  117 us
    all_to_all x1, waiting for transfers between devices, on_device(): lax.all_to_all(grad_query_h, 'seq', split_axis=0, concat_axis=1, tiled=True)  22.4 us
    all_to_all x1, waiting for transfers between devices, on_device(): lax.all_to_all(grad_out, 'seq', split_axis=1, concat_axis=0, tiled=True)  20.1 us
    all_to_all x1, waiting for transfers between devices, on_device(): lax.all_to_all(queries, 'seq', split_axis=1, concat_axis=0, tiled=True)  19 us
    dot_general x2, matrix products, step(): jnp.einsum('qngd,knd->ngqk', grad_blk, value3, preferred_element_type=jnp...  11.8 us
    all_to_all x1, starting transfers between devices, on_device(): lax.all_to_all(send_key, 'seq', split_axis=1, concat_axis=0, tiled=True)  11.1 us
    all_to_all x1, waiting for transfers between devices, on_device(): lax.all_to_all(key_grad_h, 'seq', split_axis=0, concat_axis=1, tiled=True)  10.2 us
    all_to_all x1, waiting for transfers between devices, on_device(): lax.all_to_all(value_grad_h, 'seq', split_axis=0, concat_axis=1, tiled=True)  10.2 us
  transfers between devices with their start and end apart: 8, of which 7 were waited for; matrix products, arithmetic and copies ran while one was open for 6% of the time, Pallas kernels for 0%

commit v1 on v0

--- a/solution.py
+++ b/solution.py
@@ -5,6 +5,28 @@
 from jax.sharding import PartitionSpec as P
 
 two_pi = 2.0 * math.pi
+
+
+def in_blocks(x, dim, peers):
+    before, after = (x.shape[:dim], x.shape[dim + 1 :])
+    return jnp.moveaxis(x.reshape(*before, peers, -1, *after), dim, 0)
+
+
+def joined_along(pieces, dim):
+    pieces = jnp.moveaxis(pieces, 0, dim)
+    shape = pieces.shape
+    return pieces.reshape(*shape[:dim], shape[dim] * shape[dim + 1], *shape[dim + 2 :])
+
+
+def pairwise_exchange(x, axis, split_dim, concat_dim):
+    size, index = (lax.axis_size(axis), lax.axis_index(axis))
+    parts = in_blocks(x, split_dim, size)
+    outs = [parts[index]]
+    for hop in range(1, size):
+        sent = parts[index ^ hop]
+        outs.append(lax.ppermute(sent, axis, [(i, i ^ hop) for i in range(size)]))
+    parts = jnp.stack(outs)[index ^ jnp.arange(size)]
+    return joined_along(parts, concat_dim)
 
 
 def quantize(source, clip):
@@ -118,7 +140,7 @@
     )
     attn_out, grad_queries = (
         lax.all_to_all(output_h, "seq", split_axis=0, concat_axis=1, tiled=True),
-        lax.all_to_all(grad_query_h, "seq", split_axis=0, concat_axis=1, tiled=True),
+        pairwise_exchange(grad_query_h, "seq", 0, 1),
     )
     key_gathered, value_gathered = (
         lax.all_to_all(key_grad_h, "seq", split_axis=0, concat_axis=1, tiled=True),

time: 370 us -> 355 us (0.959)
  waiting for transfers between devices: 87.9 us -> 57.3 us
  starting transfers between devices: 68.1 us -> 83.2 us
  blocking collectives: 117 us -> 110 us
  local copies, waits for them, and re-layouts: 33.1 us -> 38.3 us
    ppermute x0 -> x7, starting transfers between devices: none -> 27.2 us  [pairwise_exchange(): outs.append(lax.ppermute(sent, axis, [(i, i ^ hop) for i in range(size)]))]
    all_to_all x1 -> x0, waiting for transfers between devices: 22.4 us -> none  [on_device(): lax.all_to_all(grad_query_h, 'seq', split_axis=0, concat_axis=1, tiled=True)]
    ppermute x0 -> x7, waiting for transfers between devices: none -> 12.6 us  [pairwise_exchange(): outs.append(lax.ppermute(sent, axis, [(i, i ^ hop) for i in range(size)]))]
    all_to_all x1, waiting for transfers between devices: 10.2 us -> 0.01 us  [on_device(): lax.all_to_all(key_grad_h, 'seq', split_axis=0, concat_axis=1, tiled=True)]
    all_to_all x1, waiting for transfers between devices: 10.2 us -> 0.01 us  [on_device(): lax.all_to_all(value_grad_h, 'seq', split_axis=0, concat_axis=1, tiled=True)]
    all_to_all x1 -> x0, starting transfers between devices: 9.02 us -> none  [on_device(): lax.all_to_all(grad_query_h, 'seq', split_axis=0, concat_axis=1, tiled=True)]
    psum x1, blocking collectives: 117 us -> 110 us  [on_device(): grad_scale = lax.psum(scale_part, ('dp', 'seq'))]
    unnamed x35 -> x43, local copies, waits for them, and re-layouts: 10 us -> 12.5 us
  transfers between devices with their start and end apart: 8 -> 14, of which waited for: 7 -> 5; matrix products, arithmetic and copies ran while one was open for 6% -> 9% of each run, Pallas kernels for 0% -> 0%
where the time goes in v1:
time: 355 us; the launch traced here: 353 us
  blocking collectives  110 us (31%)
  starting transfers between devices  83.2 us (23%)
  waiting for transfers between devices  57.3 us (16%)
  matrix products  45.3 us (13%)
  local copies, waits for them, and re-layouts  38.3 us (11%)
  other arithmetic  16.2 us (5%)
    psum x1, blocking collectives, on_device(): grad_scale = lax.psum(scale_part, ('dp', 'seq'))  110 us
    ppermute x7, starting transfers between devices, pairwise_exchange(): outs.append(lax.ppermute(sent, axis, [(i, i ^ hop) for i in range(size)]))  27.2 us
    all_to_all x1, waiting for transfers between devices, on_device(): lax.all_to_all(grad_out, 'seq', split_axis=1, concat_axis=0, tiled=True)  20.1 us
    all_to_all x1, waiting for transfers between devices, on_device(): lax.all_to_all(queries, 'seq', split_axis=1, concat_axis=0, tiled=True)  19 us
    ppermute x7, waiting for transfers between devices, pairwise_exchange(): outs.append(lax.ppermute(sent, axis, [(i, i ^ hop) for i in range(size)]))  12.6 us
    unnamed x43, local copies, waits for them, and re-layouts  12.5 us
    dot_general x2, matrix products, step(): jnp.einsum('qngd,knd->ngqk', grad_blk, value3, preferred_element_type=jnp...  11.8 us
    all_to_all x1, starting transfers between devices, on_device(): lax.all_to_all(send_key, 'seq', split_axis=1, concat_axis=0, tiled=True)  11.1 us
  transfers between devices with their start and end apart: 14, of which 5 were waited for; matrix products, arithmetic and copies ran while one was open for 9% of the time, Pallas kernels for 0%

profile of v1, /device:TPU:27, one launch (start us, length us, event | category | flops | bytes accessed | tf_op | source)
XLA Modules:
  0.0 353.0 jit_solution(5655218246266364889)
XLA Ops:
  0.7 1.3 multiply_bitcast_fusion
  2.0 1.0 copy.107
  3.0 1.0 multiply_convert_fusion
  4.8 6.8 %all-to-all-start.3 = ((bf16[128,8,128]{0,2,1:T(8,128)(2,1)}), bf16[128,8,128]{0,2,1:T(8,128)(2,1)S(1)}, u32[]{:S(2)}, u32[]{:S(2)}) async-start(bf16[128,8,128]{0,2,1:T(8,128)(2,1)} %bitcast.15), calls=%async_computation.3 | async-start | bytes 524288 | tf_op jit(solution)/shard_map/all_to_all | solution.py:136
  11.6 2.3 copy.101
  13.8 5.6 %all-to-all-done.3 = bf16[128,8,128]{0,2,1:T(8,128)(2,1)S(1)} async-done(((bf16[128,8,128]{0,2,1:T(8,128)(2,1)}), bf16[128,8,128]{0,2,1:T(8,128)(2,1)S(1)}, u32[]{:S(2)}, u32[]{:S(2)}) %all-to-all-start.3) | async-done | bytes 262176 | tf_op jit(solution)/shard_map/all_to_all | solution.py:136
  19.4 6.0 %all-to-all-start = ((bf16[128,8,512]{0,2,1:T(8,128)(2,1)}), bf16[128,8,512]{0,2,1:T(8,128)(2,1)S(1)}, u32[]{:S(2)}, u32[]{:S(2)}) async-start(bf16[128,8,512]{0,2,1:T(8,128)(2,1)} %bitcast), calls=%async_computation | async-start | bytes 2097152 | tf_op jit(solution)/shard_map/all_to_all | solution.py:122
  25.4 2.3 copy.105
  27.7 19.0 %all-to-all-done = bf16[128,8,512]{0,2,1:T(8,128)(2,1)S(1)} async-done(((bf16[128,8,512]{0,2,1:T(8,128)(2,1)}), bf16[128,8,512]{0,2,1:T(8,128)(2,1)S(1)}, u32[]{:S(2)}, u32[]{:S(2)}) %all-to-all-start) | async-done | bytes 1048608 | tf_op jit(solution)/shard_map/all_to_all | solution.py:122
  46.6 9.7 %all-to-all-start.2 = ((bf16[128,8,512]{0,2,1:T(8,128)(2,1)}), bf16[128,8,512]{0,2,1:T(8,128)(2,1)S(1)}, u32[]{:S(2)}, u32[]{:S(2)}) async-start(bf16[128,8,512]{0,2,1:T(8,128)(2,1)} %bitcast.293), calls=%async_computation.2 | async-start | bytes 2097152 | tf_op jit(solution)/shard_map/all_to_all | solution.py:123
  56.5 1.0 multiply_convert_fusion.1
  57.7 20.1 %all-to-all-done.2 = bf16[128,8,512]{0,2,1:T(8,128)(2,1)S(1)} async-done(((bf16[128,8,512]{0,2,1:T(8,128)(2,1)}), bf16[128,8,512]{0,2,1:T(8,128)(2,1)S(1)}, u32[]{:S(2)}, u32[]{:S(2)}) %all-to-all-start.2) | async-done | bytes 1048608 | tf_op jit(solution)/shard_map/all_to_all | solution.py:123
  78.5 11.1 %all-to-all-start.1 = ((bf16[128,8,128]{2,0,1:T(8,128)(2,1)}), bf16[128,8,128]{2,0,1:T(8,128)(2,1)S(1)}, u32[]{:S(2)}, u32[]{:S(2)}) async-start(bf16[128,8,128]{2,0,1:T(8,128)(2,1)} %bitcast.7), calls=%async_computation.1 | async-start | bytes 524288 | tf_op jit(solution)/shard_map/all_to_all | solution.py:135
  90.1 0.9 copy.111
  91.0 1.6 copy.102
  92.6 1.5 reshape.305
  94.2 1.6 copy.106
  95.8 2.3 reshape.310
  98.1 58.9 %while.17 = (s32[]{:T(128)}, f32[1024,1,128]{0,2,1:T(8,128)S(1)}, f32[1024,1,128]{0,2,1:T(8,128)S(1)}, bf16[2,512,1,4,128]{4,3,1,0,2:T(4,128)(2,1)}, bf16[2,512,...) while((s32[]{:T(128)}, f32[1024,1,128]{0,2,1:T(8,128)S(1)}, ...), condition=%wide.region_6.7_spmd.clone, body=%wide.region_2.6_spmd.clone.sunk | while | flops 3277318656 | bytes 85563784 | solution.py:96
  100.1 1.9 fusion.74
  102.0 2.5 fusion.75
  104.5 4.0 %fusion.78 = f32[1024,1,128]{0,2,1:T(8,128)S(1)} fusion(f32[1024,1,128]{0,2,1:T(8,128)S(1)} %get-tuple-element.349, bf16[1024,1,4,128]{0,3,2,1:T(8,128)(2,1)} %get-tuple-element.371, s32[]{:T(128)S(6)} %select_n.87, pred[]{:T(512)S(6)} %compare.5, f32[4,512]{1,0:T(4,128)S(1)} %fusion.75, f32[4,512]{1,0:T(4,128)S(1)} %get-tuple-element.327, ...), kind=kOutput, calls=%fused_computation.23.clone.1 | convolution fusion | flops 547618816 | bytes 10502149 | tf_op jit(solution)/shard_map/while/body/eval_jaxpr/ngqk,qngd->knd/dot_general | solution.py:90
  108.5 4.3 %multiply_reduce_fusion.4 = (f32[512,4]{0,1:T(4,128)S(1)}, bf16[4,512,128]{1,2,0:T(8,128)(2,1)S(1)}) fusion(bf16[1024,1,4,128]{0,3,2,1:T(8,128)(2,1)} %get-tuple-element.371, s32[]{:T(128)S(6)} %select_n.87, bf16[1024,1,128]{0,2,1:T(8,128)(2,1)S(1)} %copy-done.12, f32[4,512]{1,0:T(4,128)S(1)} %fusion.75, f32[4,512]{1,0:T(4,128)S(1)} %get-tuple-element.327, ...), kind=kOutput, calls=%fused_computation.26.clone.1 | convolution fusion | flops 548665344 | bytes 10248196 | tf_op jit(solution)/shard_map/while/body/eval_jaxpr/ngqk,knd->qngd/dot_general | solution.py:76
  112.8 5.9 %fusion.76 = bf16[4,512,1024]{2,1,0:T(8,128)(2,1)} fusion(f32[4,512]{1,0:T(4,128)S(1)} %bitcast.303, f32[4,512]{1,0:T(4,128)S(1)} %fusion.75, f32[4,512]{1,0:T(4,128)S(1)} %get-tuple-element.327, f32[512,4,1024]{2,0,1:T(8,128)S(1)} %get-tuple-element.326, pred[512,1024]{1,0:T(8,128)(4,1)S(1)} %fusion.73, ...), kind=kOutput, calls=%fused_computation.11.clone.1 | convolution fusion | flops 553648128 | bytes 13918212 | tf_op jit(solution)/shard_map/while/body/eval_jaxpr/qngd,knd->ngqk/dot_general | solution.py:82
  119.1 3.2 fusion.77
  122.2 3.4 fusion.79
  126.4 0.9 copy-done.7
  129.5 1.9 fusion.74
  131.4 2.5 fusion.75
  133.9 4.0 %fusion.78 = f32[1024,1,128]{0,2,1:T(8,128)S(1)} fusion(f32[1024,1,128]{0,2,1:T(8,128)S(1)} %get-tuple-element.349, bf16[1024,1,4,128]{0,3,2,1:T(8,128)(2,1)} %get-tuple-element.371, s32[]{:T(128)S(6)} %select_n.87, pred[]{:T(512)S(6)} %compare.5, f32[4,512]{1,0:T(4,128)S(1)} %fusion.75, f32[4,512]{1,0:T(4,128)S(1)} %get-tuple-element.327, ...), kind=kOutput, calls=%fused_computation.23.clone.1 | convolution fusion | flops 547618816 | bytes 10502149 | tf_op jit(solution)/shard_map/while/body/eval_jaxpr/ngqk,qngd->knd/dot_general | solution.py:90
  137.8 4.3 %multiply_reduce_fusion.4 = (f32[512,4]{0,1:T(4,128)S(1)}, bf16[4,512,128]{1,2,0:T(8,128)(2,1)S(1)}) fusion(bf16[1024,1,4,128]{0,3,2,1:T(8,128)(2,1)} %get-tuple-element.371, s32[]{:T(128)S(6)} %select_n.87, bf16[1024,1,128]{0,2,1:T(8,128)(2,1)S(1)} %copy-done.12, f32[4,512]{1,0:T(4,128)S(1)} %fusion.75, f32[4,512]{1,0:T(4,128)S(1)} %get-tuple-element.327, ...), kind=kOutput, calls=%fused_computation.26.clone.1 | convolution fusion | flops 548665344 | bytes 10248196 | tf_op jit(solution)/shard_map/while/body/eval_jaxpr/ngqk,knd->qngd/dot_general | solution.py:76
  142.2 5.9 %fusion.76 = bf16[4,512,1024]{2,1,0:T(8,128)(2,1)} fusion(f32[4,512]{1,0:T(4,128)S(1)} %bitcast.303, f32[4,512]{1,0:T(4,128)S(1)} %fusion.75, f32[4,512]{1,0:T(4,128)S(1)} %get-tuple-element.327, f32[512,4,1024]{2,0,1:T(8,128)S(1)} %get-tuple-element.326, pred[512,1024]{1,0:T(8,128)(4,1)S(1)} %fusion.73, ...), kind=kOutput, calls=%fused_computation.11.clone.1 | convolution fusion | flops 553648128 | bytes 13918212 | tf_op jit(solution)/shard_map/while/body/eval_jaxpr/qngd,knd->ngqk/dot_general | solution.py:82
  148.4 3.2 fusion.77
  151.6 3.4 fusion.79
  155.8 0.9 copy-done.7
  157.3 1.0 copy.117
  158.2 6.8 %all-to-all-start.5 = ((f32[8,128,128]{1,2,0:T(8,128)}), f32[8,128,128]{1,2,0:T(8,128)S(1)}, u32[]{:S(2)}, u32[]{:S(2)}) async-start(f32[8,128,128]{1,2,0:T(8,128)} %copy.117), calls=%async_computation.5 | async-start | bytes 1048576 | tf_op jit(solution)/shard_map/all_to_all | solution.py:146
  165.0 1.5 reshape_reshape.2
  166.5 0.8 dynamic-slice_bitcast_fusion
  167.3 2.2 collective-permute-start
  170.1 1.3 copy.120
  171.4 1.0 copy.121
  172.4 4.3 %collective-permute-start.6 = (bf16[128,512]{1,0:T(8,128)(2,1)S(1)}, bf16[128,512]{1,0:T(8,128)(2,1)}, u32[]{:S(2)}, u32[]{:S(2)}) collective-permute-start(bf16[128,512]{1,0:T(8,128)(2,1)S(1)} %get-tuple-element.232), channel_id=1, source_target_pairs={{0,7},{1,6},{2,5},{3,4},{4,3},{5,2},{6,1},{7,0},{8,15},{9,14},{10,... | collective-permute-start | bytes 393224 | tf_op jit(solution)/shard_map/ppermute | solution.py:27
  176.7 4.0 %collective-permute-start.5 = (bf16[128,512]{1,0:T(8,128)(2,1)S(1)}, bf16[128,512]{1,0:T(8,128)(2,1)}, u32[]{:S(2)}, u32[]{:S(2)}) collective-permute-start(bf16[128,512]{1,0:T(8,128)(2,1)S(1)} %get-tuple-element.233), channel_id=1, source_target_pairs={{0,6},{1,7},{2,4},{3,5},{4,2},{5,3},{6,0},{7,1},{8,14},{9,15},{10,... | collective-permute-start | bytes 393224 | tf_op jit(solution)/shard_map/ppermute | solution.py:27
  180.7 3.4 collective-permute-start.4
  184.1 4.6 %collective-permute-start.3 = (bf16[128,512]{1,0:T(8,128)(2,1)S(1)}, bf16[128,512]{1,0:T(8,128)(2,1)S(1)}, u32[]{:S(2)}, u32[]{:S(2)}) collective-permute-start(bf16[128,512]{1,0:T(8,128)(2,1)S(1)} %get-tuple-element.235), channel_id=1, source_target_pairs={{0,4},{1,5},{2,6},{3,7},{4,0},{5,1},{6,2},{7,3},{8,12},{9,13},{10,... | collective-permute-start | bytes 393224 | tf_op jit(solution)/shard_map/ppermute | solution.py:27
  188.8 2.2 all_to_all.98
  191.0 2.5 collective-permute-start.1
  193.6 6.6 %all-to-all-start.6 = ((f32[8,128,128]{1,2,0:T(8,128)}), f32[8,128,128]{1,2,0:T(8,128)S(1)}, u32[]{:S(2)}, u32[]{:S(2)}) async-start(f32[8,128,128]{1,2,0:T(8,128)} %copy.121), calls=%async_computation.6 | async-start | bytes 1048576 | tf_op jit(solution)/shard_map/all_to_all | solution.py:147
  200.2 4.7 %collective-permute-done.1 = bf16[128,512]{1,0:T(8,128)(2,1)S(1)} collective-permute-done((bf16[128,512]{1,0:T(8,128)(2,1)}, bf16[128,512]{1,0:T(8,128)(2,1)S(1)}, u32[]{:S(2)}, u32[]{:S(2)}) %collective-permute-start.1) | collective-permute-done | bytes 131104 | tf_op jit(solution)/shard_map/ppermute | solution.py:27
  204.9 6.2 %collective-permute-start.2 = (bf16[128,512]{1,0:T(8,128)(2,1)S(1)}, bf16[128,512]{1,0:T(8,128)(2,1)S(1)}, u32[]{:S(2)}, u32[]{:S(2)}) collective-permute-start(bf16[128,512]{1,0:T(8,128)(2,1)S(1)} %get-tuple-element.236), channel_id=1, source_target_pairs={{0,3},{1,2},{2,1},{3,0},{4,7},{5,6},{6,5},{7,4},{8,11},{9,10},{10,... | collective-permute-start | bytes 393224 | tf_op jit(solution)/shard_map/ppermute | solution.py:27
  211.1 7.9 %collective-permute-done.2 = bf16[128,512]{1,0:T(8,128)(2,1)S(1)} collective-permute-done((bf16[128,512]{1,0:T(8,128)(2,1)S(1)}, bf16[128,512]{1,0:T(8,128)(2,1)S(1)}, u32[]{:S(2)}, u32[]{:S(2)}) %collective-permute-start.2) | collective-permute-done | bytes 131104 | tf_op jit(solution)/shard_map/ppermute | solution.py:27
  219.1 0.8 copy-done.1
  219.9 9.1 %all-to-all-start.4 = ((bf16[8,128,512]{2,1,0:T(8,128)(2,1)}), bf16[8,128,512]{2,1,0:T(8,128)(2,1)S(1)}, u32[]{:S(2)}, u32[]{:S(2)}) async-start(bf16[8,128,512]{2,1,0:T(8,128)(2,1)} %all_to_all.98), calls=%async_computation.4 | async-start | bytes 2097152 | tf_op jit(solution)/shard_map/all_to_all | solution.py:142
  228.9 0.9 bitcast_dynamic-update-slice_fusion.1
  229.9 0.9 bitcast_dynamic-update-slice_fusion
  232.2 1.3 copy.125
  233.5 1.1 bitcast_reduce_fusion.1
  234.6 1.1 bitcast_reduce_fusion
  235.8 3.5 %fusion.45 = (f32[512]{0:T(512)S(1)}, f32[512]{0:T(512)S(1)}, f32[128,512]{0,1:T(8,128)S(1)}, f32[512]{0:T(512)S(1)}, f32[128,512]{0,1:T(8,128)S(1)}, /*index=5*/f32[512]{0:T(512)S(1)}) fusion(f32[128,4,128]{0,2,1:T(8,128)S(1)} %bitcast_reduce_fusion, f32[512]{0:T(512)S(1)} %copy-done.15, bf16[128,512]{0,1:T(8,128)(2,1)S(1)} %copy-done.3, ...), kind=kLoop, calls=%fused_computation.51 | loop fusion | flops 2881536 | bytes 1331200 | tf_op jit(solution)/shard_map/transpose(jvp())/reduce_sum | solution.py:34
  239.5 0.8 copy.127
  240.4 0.8 copy.126
  241.2 109.9 %psum.7 = f32[2,4,128]{2,1,0:T(4,128)} all-reduce(f32[2,4,128]{2,1,0:T(4,128)S(1)} %pad_add_fusion), channel_id=1, replica_groups=mesh['dp'=64,'seq'=8] {'dp','seq'}, use_global_device_ids=true, to_apply=%region_13.14 | all-reduce | flops 1024 | bytes 8192 | tf_op jit(solution)/shard_map/psum | solution.py:152
  351.7 1.3 copy.124
  (94 shorter events, 10.5 us)
Async XLA Ops:
  0.6 55.7 %copy-start.13 = (bf16[128,512]{1,0:T(8,128)(2,1)S(1)}, bf16[128,512]{1,0:T(8,128)(2,1)}, u32[]{:S(2)}) copy-start(bf16[128,512]{1,0:T(8,128)(2,1)} %param.9) | copy-start | bytes 393220
  0.6 89.0 %copy-start.18 = (s32[1,8]{1,0:T(1,128)S(1)}, s32[1,8]{1,0:T(1,128)}, u32[]{:S(2)}) copy-start(s32[1,8]{1,0:T(1,128)} %param.13) | copy-start | bytes 100
  3.0 86.6 %copy-start.2 = (bf16[128,512]{0,1:T(8,128)(2,1)}, bf16[128,512]{0,1:T(8,128)(2,1)S(1)}, u32[]{:S(2)}) copy-start(bf16[128,512]{0,1:T(8,128)(2,1)S(1)} %copy.107) | copy-start | bytes 393220
  4.8 14.6 %all-to-all-start.3 = ((bf16[128,8,128]{0,2,1:T(8,128)(2,1)}), bf16[128,8,128]{0,2,1:T(8,128)(2,1)S(1)}, u32[]{:S(2)}, u32[]{:S(2)}) async-start(bf16[128,8,128]{0,2,1:T(8,128)(2,1)} %bitcast.15), calls=%async_computation.3 | async-start | bytes 524288 | tf_op jit(solution)/shard_map/all_to_all | solution.py:136
  19.4 27.2 %all-to-all-start = ((bf16[128,8,512]{0,2,1:T(8,128)(2,1)}), bf16[128,8,512]{0,2,1:T(8,128)(2,1)S(1)}, u32[]{:S(2)}, u32[]{:S(2)}) async-start(bf16[128,8,512]{0,2,1:T(8,128)(2,1)} %bitcast), calls=%async_computation | async-start | bytes 2097152 | tf_op jit(solution)/shard_map/all_to_all | solution.py:122
  46.6 31.2 %all-to-all-start.2 = ((bf16[128,8,512]{0,2,1:T(8,128)(2,1)}), bf16[128,8,512]{0,2,1:T(8,128)(2,1)S(1)}, u32[]{:S(2)}, u32[]{:S(2)}) async-start(bf16[128,8,512]{0,2,1:T(8,128)(2,1)} %bitcast.293), calls=%async_computation.2 | async-start | bytes 2097152 | tf_op jit(solution)/shard_map/all_to_all | solution.py:123
  56.5 33.1 %copy-start.4 = (bf16[128,512]{0,1:T(8,128)(2,1)}, bf16[128,512]{0,1:T(8,128)(2,1)S(1)}, u32[]{:S(2)}) copy-start(bf16[128,512]{0,1:T(8,128)(2,1)S(1)} %copy.103) | copy-start | bytes 393220
  78.5 19.6 %all-to-all-start.1 = ((bf16[128,8,128]{2,0,1:T(8,128)(2,1)}), bf16[128,8,128]{2,0,1:T(8,128)(2,1)S(1)}, u32[]{:S(2)}, u32[]{:S(2)}) async-start(bf16[128,8,128]{2,0,1:T(8,128)(2,1)} %bitcast.7), calls=%async_computation.1 | async-start | bytes 524288 | tf_op jit(solution)/shard_map/all_to_all | solution.py:135
  91.0 7.1 %copy-start.10 = (f32[1024,1,128]{0,2,1:T(8,128)S(1)}, f32[1024,1,128]{0,2,1:T(8,128)}, u32[]{:S(2)}) copy-start(f32[1024,1,128]{0,2,1:T(8,128)} %custom-call.1) | copy-start | bytes 1572868
  104.5 4.0 %copy-start.12 = (bf16[1024,1,128]{0,2,1:T(8,128)(2,1)S(1)}, bf16[1024,1,128]{0,2,1:T(8,128)(2,1)}, u32[]{:S(2)}) copy-start(bf16[1024,1,128]{0,2,1:T(8,128)(2,1)} %get-tuple-element.372) | copy-start | bytes 786436 | tf_op jit(solution)/shard_map/while
  119.0 6.6 %copy-start.6 = (bf16[2,512,1,4,128]{4,3,1,0,2:T(4,128)(2,1)S(1)}, bf16[2,512,1,4,128]{4,3,1,0,2:T(4,128)(2,1)}, u32[]{:S(2)}) copy-start(bf16[2,512,1,4,128]{4,3,1,0,2:T(4,128)(2,1)} %get-tuple-element.351) | copy-start | bytes 3145732 | tf_op jit(solution)/shard_map/while
  119.0 6.6 %copy-start.8 = (bf16[2,512,1,4,128]{4,3,1,0,2:T(4,128)(2,1)S(1)}, bf16[2,512,1,4,128]{4,3,1,0,2:T(4,128)(2,1)}, u32[]{:S(2)}) copy-start(bf16[2,512,1,4,128]{4,3,1,0,2:T(4,128)(2,1)} %get-tuple-element.350) | copy-start | bytes 3145732 | tf_op jit(solution)/shard_map/while
  126.4 1.0 copy-start.7
  126.4 1.3 copy-start.9
  133.8 4.0 %copy-start.12 = (bf16[1024,1,128]{0,2,1:T(8,128)(2,1)S(1)}, bf16[1024,1,128]{0,2,1:T(8,128)(2,1)}, u32[]{:S(2)}) copy-start(bf16[1024,1,128]{0,2,1:T(8,128)(2,1)} %get-tuple-element.372) | copy-start | bytes 786436 | tf_op jit(solution)/shard_map/while
  148.4 6.6 %copy-start.6 = (bf16[2,512,1,4,128]{4,3,1,0,2:T(4,128)(2,1)S(1)}, bf16[2,512,1,4,128]{4,3,1,0,2:T(4,128)(2,1)}, u32[]{:S(2)}) copy-start(bf16[2,512,1,4,128]{4,3,1,0,2:T(4,128)(2,1)} %get-tuple-element.351) | copy-start | bytes 3145732 | tf_op jit(solution)/shard_map/while
  148.4 6.6 %copy-start.8 = (bf16[2,512,1,4,128]{4,3,1,0,2:T(4,128)(2,1)S(1)}, bf16[2,512,1,4,128]{4,3,1,0,2:T(4,128)(2,1)}, u32[]{:S(2)}) copy-start(bf16[2,512,1,4,128]{4,3,1,0,2:T(4,128)(2,1)} %get-tuple-element.350) | copy-start | bytes 3145732 | tf_op jit(solution)/shard_map/while
  155.7 1.0 copy-start.7
  155.8 1.3 copy-start.9
  157.1 8.0 %copy-start.11 = (f32[1024,1,128]{0,2,1:T(8,128)}, f32[1024,1,128]{0,2,1:T(8,128)S(1)}, u32[]{:S(2)}) copy-start(f32[1024,1,128]{0,2,1:T(8,128)S(1)} %get-tuple-element.73) | copy-start | bytes 1572868
  158.2 35.3 %all-to-all-start.5 = ((f32[8,128,128]{1,2,0:T(8,128)}), f32[8,128,128]{1,2,0:T(8,128)S(1)}, u32[]{:S(2)}, u32[]{:S(2)}) async-start(f32[8,128,128]{1,2,0:T(8,128)} %copy.117), calls=%async_computation.5 | async-start | bytes 1048576 | tf_op jit(solution)/shard_map/all_to_all | solution.py:146
  167.3 23.7 %collective-permute-start = (bf16[128,512]{1,0:T(8,128)(2,1)}, bf16[128,512]{1,0:T(8,128)(2,1)S(1)}, u32[]{:S(2)}, u32[]{:S(2)}) collective-permute-start(bf16[128,512]{1,0:T(8,128)(2,1)} %get-tuple-element.238), channel_id=1, source_target_pairs={{0,1},{1,0},{2,3},{3,2},{4,5},{5,4},{6,7},{7,6},{8,9},{9,8},{10,11... | collective-permute-start | bytes 393224 | tf_op jit(solution)/shard_map/ppermute | solution.py:27
  170.1 65.6 %copy-start.3 = (bf16[128,512]{0,1:T(8,128)(2,1)S(1)}, bf16[128,512]{0,1:T(8,128)(2,1)}, u32[]{:S(2)}) copy-start(bf16[128,512]{0,1:T(8,128)(2,1)} %copy-done.2) | copy-start | bytes 393220
  170.1 65.6 %copy-start.5 = (bf16[128,512]{0,1:T(8,128)(2,1)S(1)}, bf16[128,512]{0,1:T(8,128)(2,1)}, u32[]{:S(2)}) copy-start(bf16[128,512]{0,1:T(8,128)(2,1)} %copy-done.4) | copy-start | bytes 393220
  170.1 65.6 %copy-start.14 = (f32[512]{0:T(512)S(1)}, f32[512]{0:T(512)}, u32[]{:S(2)}) copy-start(f32[512]{0:T(512)} %get-tuple-element.242) | copy-start | bytes 6148
  170.1 65.7 %copy-start.15 = (f32[512]{0:T(512)S(1)}, f32[512]{0:T(512)}, u32[]{:S(2)}) copy-start(f32[512]{0:T(512)} %get-tuple-element.246) | copy-start | bytes 6148
  170.1 65.7 %copy-start.16 = (f32[512]{0:T(512)S(1)}, f32[512]{0:T(512)}, u32[]{:S(2)}) copy-start(f32[512]{0:T(512)} %get-tuple-element.240) | copy-start | bytes 6148
  170.1 65.7 %copy-start.17 = (f32[512]{0:T(512)S(1)}, f32[512]{0:T(512)}, u32[]{:S(2)}) copy-start(f32[512]{0:T(512)} %get-tuple-element.243) | copy-start | bytes 6148
  172.4 57.5 %collective-permute-start.6 = (bf16[128,512]{1,0:T(8,128)(2,1)S(1)}, bf16[128,512]{1,0:T(8,128)(2,1)}, u32[]{:S(2)}, u32[]{:S(2)}) collective-permute-start(bf16[128,512]{1,0:T(8,128)(2,1)S(1)} %get-tuple-element.232), channel_id=1, source_target_pairs={{0,7},{1,6},{2,5},{3,4},{4,3},{5,2},{6,1},{7,0},{8,15},{9,14},{10,... | collective-permute-start | bytes 393224 | tf_op jit(solution)/shard_map/ppermute | solution.py:27
  176.7 52.2 %collective-permute-start.5 = (bf16[128,512]{1,0:T(8,128)(2,1)S(1)}, bf16[128,512]{1,0:T(8,128)(2,1)}, u32[]{:S(2)}, u32[]{:S(2)}) collective-permute-start(bf16[128,512]{1,0:T(8,128)(2,1)S(1)} %get-tuple-element.233), channel_id=1, source_target_pairs={{0,6},{1,7},{2,4},{3,5},{4,2},{5,3},{6,0},{7,1},{8,14},{9,15},{10,... | collective-permute-start | bytes 393224 | tf_op jit(solution)/shard_map/ppermute | solution.py:27
  180.7 38.3 %collective-permute-start.4 = (bf16[128,512]{1,0:T(8,128)(2,1)S(1)}, bf16[128,512]{1,0:T(8,128)(2,1)S(1)}, u32[]{:S(2)}, u32[]{:S(2)}) collective-permute-start(bf16[128,512]{1,0:T(8,128)(2,1)S(1)} %get-tuple-element.234), channel_id=1, source_target_pairs={{0,5},{1,4},{2,7},{3,6},{4,1},{5,0},{6,3},{7,2},{8,13},{9,12},{10,... | collective-permute-start | bytes 393224 | tf_op jit(solution)/shard_map/ppermute | solution.py:27
  184.1 34.9 %collective-permute-start.3 = (bf16[128,512]{1,0:T(8,128)(2,1)S(1)}, bf16[128,512]{1,0:T(8,128)(2,1)S(1)}, u32[]{:S(2)}, u32[]{:S(2)}) collective-permute-start(bf16[128,512]{1,0:T(8,128)(2,1)S(1)} %get-tuple-element.235), channel_id=1, source_target_pairs={{0,4},{1,5},{2,6},{3,7},{4,0},{5,1},{6,2},{7,3},{8,12},{9,13},{10,... | collective-permute-start | bytes 393224 | tf_op jit(solution)/shard_map/ppermute | solution.py:27
  191.0 13.9 %collective-permute-start.1 = (bf16[128,512]{1,0:T(8,128)(2,1)}, bf16[128,512]{1,0:T(8,128)(2,1)S(1)}, u32[]{:S(2)}, u32[]{:S(2)}) collective-permute-start(bf16[128,512]{1,0:T(8,128)(2,1)} %get-tuple-element.237), channel_id=1, source_target_pairs={{0,2},{1,3},{2,0},{3,1},{4,6},{5,7},{6,4},{7,5},{8,10},{9,11},{10,... | collective-permute-start | bytes 393224 | tf_op jit(solution)/shard_map/ppermute | solution.py:27
  193.6 36.3 %copy-start = (f32[8,128,128]{1,2,0:T(8,128)}, f32[8,128,128]{1,2,0:T(8,128)S(1)}, u32[]{:S(2)}) copy-start(f32[8,128,128]{1,2,0:T(8,128)S(1)} %all-to-all-done.5) | copy-start | bytes 1572868
  193.6 25.5 %all-to-all-start.6 = ((f32[8,128,128]{1,2,0:T(8,128)}), f32[8,128,128]{1,2,0:T(8,128)S(1)}, u32[]{:S(2)}, u32[]{:S(2)}) async-start(f32[8,128,128]{1,2,0:T(8,128)} %copy.121), calls=%async_computation.6 | async-start | bytes 1048576 | tf_op jit(solution)/shard_map/all_to_all | solution.py:147
  204.9 14.1 %collective-permute-start.2 = (bf16[128,512]{1,0:T(8,128)(2,1)S(1)}, bf16[128,512]{1,0:T(8,128)(2,1)S(1)}, u32[]{:S(2)}, u32[]{:S(2)}) collective-permute-start(bf16[128,512]{1,0:T(8,128)(2,1)S(1)} %get-tuple-element.236), channel_id=1, source_target_pairs={{0,3},{1,2},{2,1},{3,0},{4,7},{5,6},{6,5},{7,4},{8,11},{9,10},{10,... | collective-permute-start | bytes 393224 | tf_op jit(solution)/shard_map/ppermute | solution.py:27
  219.1 0.8 copy-start.1
  219.9 131.2 %all-to-all-start.4 = ((bf16[8,128,512]{2,1,0:T(8,128)(2,1)}), bf16[8,128,512]{2,1,0:T(8,128)(2,1)S(1)}, u32[]{:S(2)}, u32[]{:S(2)}) async-start(bf16[8,128,512]{2,1,0:T(8,128)(2,1)} %all_to_all.98), calls=%async_computation.4 | async-start | bytes 2097152 | tf_op jit(solution)/shard_map/all_to_all | solution.py:142
